TPU v7x, 32 devices: a whole 2x2x4 slice. The times are simulated.
32 devices in a mesh: space: 8 (over y, x, core), chan: 4 (over z).
Axes of the slice: x: 2, y: 2, z: 4, core: 2. Of those that a mesh axis runs over, the one named last changes fastest.
Arguments:
- activation: bfloat16 [8, 96, 16, 128], P('space', 'chan'), may hold values from -6 to 6
- weights: bfloat16 [3, 3, 3, 96, 96], replicated, may hold values from -0.125 to 0.125
- cotangent: bfloat16 [8, 96, 16, 128], P('space', 'chan'), may hold values from -6 to 6
Outputs:
- output: bfloat16 [8, 96, 16, 128], P('space', 'chan')
- input_grad: bfloat16 [8, 96, 16, 128], P('space', 'chan')
- weight_grad: float32 [3, 3, 3, 96, 96], P(None, None, None, None, 'chan')
All inputs are finite; a program needn't handle non-finite values.
Results may differ from a plain program's by a relative error of at most 0.0095.
Values may be sent and summed in bfloat16 or wider, within the bound.
A program may use at most 64 MiB of HBM per device.

v0:
```python
import functools
import math

import jax
import jax.numpy as jnp
from jax import lax
from jax.experimental import pallas as pl
from jax.experimental.pallas import tpu as pltpu
from jax.sharding import PartitionSpec as P

BF, F32 = jnp.bfloat16, jnp.float32
LANE = 128


def kernel(space, chan, blk, pad, channels, height, scale,
           a_ref, g_ref, w_ref, out_ref, back_ref, wg_ref,
           ga, x3, xg, wf, wb, s32, t32, r32, z32, part,
           halo, psend, precv, wflat, wsend, wrecv, wfull,
           rsend, rrecv,
           g_s, g_r, h_s, h_r, p_s, p_r, w_s, w_r, f_s, f_r, r_s, r_r):
    e = lax.axis_index("space")
    z = lax.axis_index("chan")
    rows = blk * height
    span = height * LANE
    up, down = lax.rem(e + 1, space), lax.rem(e + space - 1, space)

    def along_z(k):
        return lax.rem(z + k, chan)

    def along_e(k):
        return lax.rem(e + k, space)

    barrier = pltpu.get_barrier_semaphore()
    others = [{"chan": along_z(k)} for k in range(1, chan)]
    others += [{"space": along_e(k)} for k in range(1, space)]
    for other in others:
        pl.semaphore_signal(barrier, inc=1, device_id=other)
    pl.semaphore_wait(barrier, len(others))

    def send(src, dst, ssem, rsem, to):
        return pltpu.make_async_remote_copy(src, dst, ssem, rsem, device_id=to)

    gathers = [send(a_ref, ga.at[z], g_s.at[k], g_r.at[k], {"chan": along_z(k)})
               for k in range(1, chan)]

    halo_up = send(g_ref, halo.at[0], h_s.at[0], h_r.at[0], {"space": up})
    halo_down = send(g_ref, halo.at[1], h_s.at[1], h_r.at[1], {"space": down})
    has_up, has_down = e < space - 1, e > 0

    for c in gathers:
        c.start()
    pl.when(has_up)(halo_up.start)
    pl.when(has_down)(halo_down.start)

    def no_lower():
        halo[0] = jnp.zeros((rows, LANE), BF)
        precv[0] = jnp.zeros((rows, LANE), BF)

    def no_upper():
        halo[1] = jnp.zeros((rows, LANE), BF)
        precv[1] = jnp.zeros((rows, LANE), BF)

    pl.when(e == 0)(no_lower)
    pl.when(e == space - 1)(no_upper)
    ga[z] = a_ref[...]

    wide = 9 * pad
    first = lax.broadcasted_iota(jnp.int32, (channels, wide), 0) - z * blk
    place = lax.broadcasted_iota(jnp.int32, (channels, wide), 1)
    inside = (first >= 0) & (first < blk)
    for b in range(3):
        total = jnp.zeros((channels, wide), F32)
        for c in range(3):
            for a in range(3):
                spot = inside & (place == first + (c * 3 + a) * pad)
                tap = w_ref[(a * 3 + 2 - b) * 3 + 2 - c]
                total = total + jnp.dot(
                    tap, jnp.where(spot, 1.0, 0.0).astype(BF), preferred_element_type=F32)
        wb[b * channels:(b + 1) * channels, :] = total.astype(BF)

    z32[...] = jnp.zeros_like(z32)
    few = lax.broadcasted_iota(jnp.int32, (rows, LANE), 1)

    def fill(a, src):
        v = src.astype(F32)
        z32[0, 0:rows, :] = jnp.where(few == 0, 0.0, pltpu.roll(v, 1, 1))
        z32[1, 0:rows, :] = v
        z32[2, 0:rows, :] = jnp.where(few == LANE - 1, 0.0, pltpu.roll(v, LANE - 1, 1))
        for c in range(3):
            at = (c * 3 + a) * pad
            for h in range(height):
                xg[at:at + pad, h * LANE:(h + 1) * LANE] = (
                    z32[c, pl.ds(h, pad, stride=height), :].astype(BF))

    fill(1, g_ref[...])
    pl.when(has_down)(halo_up.wait_recv)
    fill(2, halo[0])
    pl.when(has_up)(halo_down.wait_recv)
    fill(0, halo[1])

    def shifted(count, first_row, group, h):
        def piece(b, hh):
            at = first_row + b * group
            return r32[at:at + count, hh * LANE:(hh + 1) * LANE]
        v = piece(1, h)
        if h > 0:
            v = v + piece(0, h - 1)
        if h < height - 1:
            v = v + piece(2, h + 1)
        return v

    r32[0:3 * channels, :] = jnp.dot(wb[...], xg[...], preferred_element_type=F32)
    for h in range(height):
        part[pl.ds(h, channels, stride=height), :] = shifted(channels, 0, channels, h)

    sums = [send(rsend.at[k], rrecv.at[k], r_s.at[k], r_r.at[k], {"chan": along_z(k)})
            for k in range(1, chan)]

    def block(t):
        return part[pl.ds(pl.multiple_of(t * rows, 16), rows), :]

    for k in range(1, chan):
        rsend[k] = block(along_z(k)).astype(BF)

    x3[...] = jnp.zeros_like(x3)
    wf[...] = jnp.zeros_like(wf)
    row = lax.broadcasted_iota(jnp.int32, (pad, channels), 0)
    col = lax.broadcasted_iota(jnp.int32, (pad, channels), 1)
    pick = jnp.where((col == row + z * blk) & (row < blk), 1.0, 0.0).astype(BF)
    for a in range(3):
        for b in range(3):
            for c in range(3):
                wf[pl.ds((b * 3 + a) * pad, pad), pl.ds(c * LANE, channels)] = (
                    lax.dot_general(
                        pick, w_ref[(a * 3 + b) * 3 + c], (((1,), (1,)), ((), ())),
                        preferred_element_type=F32).astype(BF))

    for c in gathers:
        c.wait_recv()
    for c in sums:
        c.start()
    lane = lax.broadcasted_iota(jnp.int32, (channels * height, LANE), 1)
    v = ga[...].reshape(channels * height, LANE).astype(F32)
    s32[0] = jnp.where(lane == 0, 0.0, pltpu.roll(v, 1, 1))
    s32[1] = v
    s32[2] = jnp.where(lane == LANE - 1, 0.0, pltpu.roll(v, LANE - 1, 1))
    for c in range(3):
        for h in range(height):
            x3[c * LANE:c * LANE + channels, (h + 1) * LANE:(h + 2) * LANE] = (
                s32[c, pl.ds(h, channels, stride=height), :].astype(BF))

    signal = xg[3 * pad:6 * pad, :]
    for b in range(3):
        share = lax.dot_general(
            signal, x3[:, b * LANE:b * LANE + span], (((1,), (1,)), ((), ())),
            preferred_element_type=F32)
        for c in range(3):
            at = (c * 9 + b * 3) * pad
            wflat[at:at + 3 * pad, :] = share[:, c * LANE:(c + 1) * LANE]
    total_rows = wflat.shape[0]
    chunk = total_rows // space
    if total_rows > 27 * pad:
        wflat[27 * pad:total_rows, :] = jnp.zeros((total_rows - 27 * pad, LANE), F32)
    wsend[...] = wflat[...].astype(BF).reshape(space, chunk, LANE)
    shares = [send(wsend.at[along_e(k)], wrecv.at[k], w_s.at[k], w_r.at[k],
                   {"space": along_e(k)}) for k in range(1, space)]
    for c in shares:
        c.start()

    r32[0:9 * pad, :] = jnp.dot(wf[...], x3[:, LANE:LANE + span], preferred_element_type=F32)

    def relay(a):
        for h in range(height):
            t32[a, pl.ds(h, pad, stride=height), :] = shifted(pad, a * pad, 3 * pad, h)

    relay(0)
    psend[0] = t32[0, 0:rows, :].astype(BF)
    pair = (send(psend.at[0], precv.at[0], p_s.at[0], p_r.at[0], {"space": up}),
            send(psend.at[1], precv.at[1], p_s.at[1], p_r.at[1], {"space": down}))
    pl.when(has_up)(pair[0].start)
    relay(2)
    psend[1] = t32[2, 0:rows, :].astype(BF)
    pl.when(has_down)(pair[1].start)

    relay(1)
    for c in shares:
        c.wait_recv()
    mine = wflat[pl.ds(pl.multiple_of(e * chunk, 16), chunk), :]
    for k in range(1, space):
        mine = mine + wrecv[k].astype(F32)
    wfull[e] = mine.astype(BF)
    fulls = [send(wfull.at[e], wfull.at[e], f_s.at[k], f_r.at[k], {"space": along_e(k)})
             for k in range(1, space)]
    for c in fulls:
        c.start()

    pl.when(has_down)(pair[0].wait_recv)
    pl.when(has_up)(pair[1].wait_recv)
    out_ref[...] = (t32[1, 0:rows, :] + precv[0].astype(F32)
                    + precv[1].astype(F32)).astype(BF)

    for c in sums:
        c.wait_recv()
    total = block(z)
    for k in range(1, chan):
        total = total + rrecv[k].astype(F32)
    back_ref[...] = total.astype(BF)

    for c in fulls:
        c.wait_recv()
    wflat[...] = wfull[...].reshape(total_rows, LANE).astype(F32) * scale
    for a in range(3):
        for b in range(3):
            for c in range(3):
                at = (c * 9 + b * 3 + a) * pad
                wg_ref[(a * 3 + b) * 3 + c] = wflat[at:at + blk, 0:channels]

    for c in gathers + sums + shares + fulls:
        c.wait_send()
    for c in (halo_up, pair[0]):
        pl.when(has_up)(c.wait_send)
    for c in (halo_down, pair[1]):
        pl.when(has_down)(c.wait_send)


def body(space, chan, activation, weights, cotangent):
    planes, blk, height, width = activation.shape
    channels = weights.shape[3]
    assert planes == 1 and width == LANE
    pad = -(-blk // 16) * 16
    rows = blk * height
    scale = 1.0 / math.sqrt(planes * space * height * width)
    dma = pltpu.SemaphoreType.DMA
    vm = pltpu.VMEM
    wide = (height + 2) * LANE
    chunk = -(-27 * pad // (16 * space)) * 16
    out, back, grads = pl.pallas_call(
        functools.partial(kernel, space, chan, blk, pad, channels, height, scale),
        out_shape=(
            jax.ShapeDtypeStruct((rows, LANE), BF),
            jax.ShapeDtypeStruct((rows, LANE), BF),
            jax.ShapeDtypeStruct((27, blk, channels), F32),
        ),
        in_specs=[pl.BlockSpec(memory_space=pltpu.VMEM)] * 3,
        out_specs=[pl.BlockSpec(memory_space=pltpu.VMEM)] * 3,
        scratch_shapes=[
            vm((chan, rows, LANE), BF),
            vm((3 * LANE, wide), BF),
            vm((9 * pad, height * LANE), BF),
            vm((9 * pad, 3 * LANE), BF),
            vm((3 * channels, 9 * pad), BF),
            vm((3, channels * height, LANE), F32),
            vm((3, pad * height, LANE), F32),
            vm((max(9 * pad, 3 * channels), height * LANE), F32),
            vm((3, pad * height, LANE), F32),
            vm((channels * height, LANE), F32),
            vm((2, rows, LANE), BF),
            vm((2, rows, LANE), BF),
            vm((2, rows, LANE), BF),
            vm((space * chunk, LANE), F32),
            vm((space, chunk, LANE), BF),
            vm((space, chunk, LANE), BF),
            vm((space, chunk, LANE), BF),
            vm((chan, rows, LANE), BF),
            vm((chan, rows, LANE), BF),
            dma((chan,)), dma((chan,)), dma((2,)), dma((2,)), dma((2,)), dma((2,)),
            dma((space,)), dma((space,)), dma((space,)), dma((space,)),
            dma((chan,)), dma((chan,)),
        ],
        compiler_params=pltpu.CompilerParams(
            collective_id=0, has_side_effects=True, vmem_limit_bytes=40 * 2**20),
    )(activation.reshape(rows, width), cotangent.reshape(rows, width),
      weights.reshape(27, channels, channels))
    field = (1, blk, height, width)
    grads = jnp.swapaxes(grads.reshape(3, 3, 3, blk, channels), 3, 4)
    return out.reshape(field), back.reshape(field), grads


def solution(mesh):
    field = P("space", "chan", None, None)
    return jax.shard_map(
        functools.partial(body, mesh.shape["space"], mesh.shape["chan"]),
        mesh=mesh,
        in_specs=(field, P(), field),
        out_specs=(field, field, P(None, None, None, None, "chan")),
        check_vma=False,
    )
```

profile of v0, /device:TPU:0, one launch (start us, length us, event | category | flops | bytes accessed | tf_op | source)
XLA Modules:
  0.0 31.3 jit_solution(4233962289419288722)
XLA Ops:
  0.6 0.0 copy-start
  0.6 1.1 %copy-done = bf16[3,3,3,96,96]{4,3,2,1,0:T(8,128)(2,1)S(1)} copy-done((bf16[3,3,3,96,96]{4,3,2,1,0:T(8,128)(2,1)S(1)}, bf16[3,3,3,96,96]{4,3,2,1,0:T(8,128)(2,1)}, u32[]{:S(2)}) %copy-start) | copy-done | bytes 497688
  1.7 0.0 copy-start.1
  1.7 0.9 %copy-done.1 = bf16[1,24,16,128]{3,2,1,0:T(8,128)(2,1)S(1)} copy-done((bf16[1,24,16,128]{3,2,1,0:T(8,128)(2,1)S(1)}, bf16[1,24,16,128]{3,2,1,0:T(8,128)(2,1)}, u32[]{:S(2)}) %copy-start.1) | copy-done | bytes 98328
  2.6 0.0 copy-start.2
  2.6 0.9 %copy-done.2 = bf16[1,24,16,128]{3,2,1,0:T(8,128)(2,1)S(1)} copy-done((bf16[1,24,16,128]{3,2,1,0:T(8,128)(2,1)S(1)}, bf16[1,24,16,128]{3,2,1,0:T(8,128)(2,1)}, u32[]{:S(2)}) %copy-start.2) | copy-done | bytes 98328
  3.5 25.8 %shard_map.58 = (bf16[384,128]{1,0:T(8,128)(2,1)S(1)}, bf16[384,128]{1,0:T(8,128)(2,1)S(1)}, f32[27,24,96]{2,1,0:T(8,128)S(1)}) custom-call(bf16[384,128]{1,0:T(8,128)(2,1)S(1)} %bitcast.12, bf16[384,128]{1,0:T(8,128)(2,1)S(1)} %bitcast.13, bf16[27,96,96]{2,1,0:T(8,128)(2,1)S(1)} %bitcast.8), custom_call_target="tpu_custom_call" | custom-call | tf_op jit(solution)/shard_map/pallas_call | solution.py:237
  29.3 0.6 %copy.9 = bf16[1,24,16,128]{3,2,1,0:T(8,128)(2,1)} copy(bf16[1,24,16,128]{3,2,1,0:T(8,128)(2,1)S(1)} %bitcast.11) | data formatting | bytes 196608
  29.9 0.6 %copy.10 = bf16[1,24,16,128]{3,2,1,0:T(8,128)(2,1)} copy(bf16[1,24,16,128]{3,2,1,0:T(8,128)(2,1)S(1)} %bitcast.10) | data formatting | bytes 196608
  30.6 0.7 %copy.11 = f32[3,3,3,96,24]{3,4,2,1,0:T(8,128)} copy(f32[3,3,3,96,24]{3,4,2,1,0:T(8,128)S(1)} %bitcast.9) | data formatting | bytes 497664
Async XLA Ops:
  0.6 1.1 %copy-start = (bf16[3,3,3,96,96]{4,3,2,1,0:T(8,128)(2,1)S(1)}, bf16[3,3,3,96,96]{4,3,2,1,0:T(8,128)(2,1)}, u32[]{:S(2)}) copy-start(bf16[3,3,3,96,96]{4,3,2,1,0:T(8,128)(2,1)} %param.4) | copy-start | bytes 1492996
  1.7 0.9 %copy-start.1 = (bf16[1,24,16,128]{3,2,1,0:T(8,128)(2,1)S(1)}, bf16[1,24,16,128]{3,2,1,0:T(8,128)(2,1)}, u32[]{:S(2)}) copy-start(bf16[1,24,16,128]{3,2,1,0:T(8,128)(2,1)} %param.3) | copy-start | bytes 294916
  2.6 0.9 %copy-start.2 = (bf16[1,24,16,128]{3,2,1,0:T(8,128)(2,1)S(1)}, bf16[1,24,16,128]{3,2,1,0:T(8,128)(2,1)}, u32[]{:S(2)}) copy-start(bf16[1,24,16,128]{3,2,1,0:T(8,128)(2,1)} %param.5) | copy-start | bytes 294916
where the time goes:
time: 31.5 us; the launch traced here: 31.3 us
  Pallas kernels  25.8 us (82%)
  local copies, waits for them, and re-layouts  4.88 us (15%)
  between operations  0.65 us (2%)
    pallas_call x1, Pallas kernels, body(): pl.pallas_call(functools.partial(kernel, space, chan, blk, pad, channels,...  25.8 us
    unnamed x9, local copies, waits for them, and re-layouts  4.88 us

commit v1 on v0

v1 whole, which is shorter than its diff:
```python
import functools
import math

import jax
import jax.numpy as jnp
from jax import lax
from jax.experimental import pallas as pl
from jax.experimental.pallas import tpu as pltpu
from jax.sharding import PartitionSpec as P

BF, F32 = jnp.bfloat16, jnp.float32
LANE = 128
ROWS_T = (((1,), (1,)), ((), ()))


def up_to(n, m):
    return -(-n // m) * m


def flip(i, m):
    out = i
    for b in range(m.bit_length()):
        if m >> b & 1:
            bit = lax.rem(lax.div(i, 1 << b), 2)
            out = out + (1 << b) * (1 - 2 * bit)
    return out


def kernel(space, chan, blk, pad, channels, height, groups, scale,
           a_hbm, g_hbm, w_hbm, out_ref, back_ref, wg_ref,
           ga, gv, w_ref, x3, xg, wt, wf, wb, z32, t32, r32, part,
           halo, psend, precv, wflat, csend, crecv, wall, acc, place_q,
           rsend, rrecv,
           l_s, g_s, g_r, h_s, h_r, p_s, p_r, c_s, c_r, w_s, w_r, r_s, r_r):
    e = lax.axis_index("space")
    z = lax.axis_index("chan")
    rows = blk * height
    span = height * LANE
    per = chan // groups
    half, gl = wall.shape[2], wall.shape[3]
    some = -(-blk // 8) * 8
    wide = acc.shape[1] // 3
    up, down = lax.rem(e + 1, space), lax.rem(e + space - 1, space)
    core = lax.rem(e, 2)

    barrier = pltpu.get_barrier_semaphore()
    others = [{"chan": flip(z, k)} for k in range(1, chan)]
    others += [{"space": flip(e, k)} for k in range(1, space)]
    for other in others:
        pl.semaphore_signal(barrier, inc=1, device_id=other)
    loads = [pltpu.make_async_copy(g_hbm, gv, l_s.at[0]),
             pltpu.make_async_copy(a_hbm, ga.at[0], l_s.at[1]),
             pltpu.make_async_copy(w_hbm, w_ref, l_s.at[2])]
    for c in loads:
        c.start()

    def send(src, dst, ssem, rsem, to):
        return pltpu.make_async_remote_copy(src, dst, ssem, rsem, device_id=to)

    gathers = [None] + [
        send(a_hbm, ga.at[k], g_s.at[k], g_r.at[k], {"chan": flip(z, k)})
        for k in range(1, chan)]
    halo_up = send(g_hbm, halo.at[0], h_s.at[0], h_r.at[0], {"space": up})
    halo_down = send(g_hbm, halo.at[1], h_s.at[1], h_r.at[1], {"space": down})
    has_up, has_down = e < space - 1, e > 0

    pl.semaphore_wait(barrier, len(others))
    for c in gathers[1:]:
        c.start()
    pl.when(has_up)(halo_up.start)
    pl.when(has_down)(halo_down.start)

    def no_lower():
        halo[0] = jnp.zeros((rows, LANE), BF)
        precv[0] = jnp.zeros((rows, LANE), BF)

    def no_upper():
        halo[1] = jnp.zeros((rows, LANE), BF)
        precv[1] = jnp.zeros((rows, LANE), BF)

    pl.when(e == 0)(no_lower)
    pl.when(e == space - 1)(no_upper)

    z32[...] = jnp.zeros_like(z32)
    x3[:, 0:LANE] = jnp.zeros((x3.shape[0], LANE), BF)
    x3[:, span + LANE:span + 2 * LANE] = jnp.zeros((x3.shape[0], LANE), BF)
    wflat[...] = jnp.zeros_like(wflat)
    few = lax.broadcasted_iota(jnp.int32, (rows, LANE), 1)

    def fill(dst, row_of, first, src):
        v = src.astype(F32)
        z32[0, 0:rows, :] = jnp.where(few == 0, 0.0, pltpu.roll(v, 1, 1))
        z32[1, 0:rows, :] = v
        z32[2, 0:rows, :] = jnp.where(few == LANE - 1, 0.0, pltpu.roll(v, LANE - 1, 1))
        for c in range(3):
            at = row_of(c)
            for h in range(height):
                dst[at:at + pad, (h + first) * LANE:(h + first + 1) * LANE] = (
                    z32[c, pl.ds(h, pad, stride=height), :].astype(BF))

    def fill_signal(a, src):
        fill(xg, lambda c: (c * 3 + a) * pad, 0, src)

    def fill_source(k):
        fill(x3, lambda c: (k * 3 + c) * pad, 1, ga[k])

    loads[0].wait()
    fill_signal(1, gv[...])
    loads[1].wait()
    fill_source(0)

    loads[2].wait()
    thick = 9 * pad
    first = lax.broadcasted_iota(jnp.int32, (channels, thick), 0) - z * blk
    place = lax.broadcasted_iota(jnp.int32, (channels, thick), 1)
    inside = (first >= 0) & (first < blk)
    for b in range(3):
        total = jnp.zeros((channels, thick), F32)
        for c in range(3):
            for a in range(3):
                spot = inside & (place == first + (c * 3 + a) * pad)
                tap = w_ref[(a * 3 + 2 - b) * 3 + 2 - c]
                total = total + jnp.dot(
                    tap, jnp.where(spot, 1.0, 0.0).astype(BF), preferred_element_type=F32)
        wb[b * channels:(b + 1) * channels, :] = total.astype(BF)

    row = lax.broadcasted_iota(jnp.int32, (pad, channels), 0)
    col = lax.broadcasted_iota(jnp.int32, (pad, channels), 1)
    pick = jnp.where((col == row + z * blk) & (row < blk), 1.0, 0.0).astype(BF)
    for a in range(3):
        for b in range(3):
            for c in range(3):
                at = (b * 3 + a) * pad
                wt[c, at:at + pad, :] = lax.dot_general(
                    pick, w_ref[(a * 3 + b) * 3 + c], ROWS_T,
                    preferred_element_type=F32).astype(BF)
    deep = 3 * pad * chan
    channel = lax.broadcasted_iota(jnp.int32, (channels, deep), 0)
    spot = lax.broadcasted_iota(jnp.int32, (channels, deep), 1)
    goes = jnp.zeros((channels, deep), jnp.int32)
    for k in range(chan):
        local = channel - flip(z, k) * blk
        goes = jnp.where((local >= 0) & (local < blk), local + k * 3 * pad, goes)
    total = jnp.zeros((9 * pad, deep), F32)
    for c in range(3):
        total = total + jnp.dot(
            wt[c], jnp.where(spot == goes + c * pad, 1.0, 0.0).astype(BF),
            preferred_element_type=F32)
    wf[...] = total.astype(BF)

    place_q[...] = jnp.zeros_like(place_q)
    row = lax.broadcasted_iota(jnp.int32, (pad, wide), 0)
    col = lax.broadcasted_iota(jnp.int32, (pad, wide), 1)
    for k in range(chan):
        hit = (row < blk) & (col == row + flip(z, k) * blk)
        block = jnp.where(hit, 1.0, 0.0).astype(BF)
        for c in range(3):
            at = ((k % per) * 3 + c) * pad
            place_q[k // per, at:at + pad, c * wide:(c + 1) * wide] = block

    pairs = [send(csend.at[k], crecv.at[k], c_s.at[k], c_r.at[k], {"space": flip(e, 1)})
             for k in range(groups)]
    shares = [[send(wall.at[k, e], wall.at[k, e], w_s.at[k, m], w_r.at[k, m],
                    {"space": flip(e, m)}) for m in range(1, space)]
              for k in range(groups)]

    def my_half(k, which):
        return wflat[k, pl.ds(pl.multiple_of(which * half, 16), half), :]

    def share(k):
        many = per * 3 * pad
        for b in range(3):
            one = lax.dot_general(
                xg[3 * pad:6 * pad, :],
                x3[k * many:(k + 1) * many, b * LANE:b * LANE + span],
                ROWS_T, preferred_element_type=F32)
            for a in range(3):
                at = (b * 3 + a) * some
                wflat[k, at:at + some, 0:many] = one[a * pad:a * pad + some, :]
        csend[k] = my_half(k, 1 - core).astype(BF)
        pairs[k].start()

    def spread(k):
        pairs[k].wait_recv()
        wall[k, e] = (my_half(k, core) + crecv[k].astype(F32)).astype(BF)
        for c in shares[k]:
            c.start()

    def collect(k):
        for c in shares[k]:
            c.wait_recv()
        for side in range(2):
            total = wall[k, side].astype(F32)
            for chip in range(1, space // 2):
                total = total + wall[k, 2 * chip + side].astype(F32)
            moved = jnp.dot(total.astype(BF), place_q[k], preferred_element_type=F32)
            at = side * half
            acc[at:at + half, :] = moved if k == 0 else acc[at:at + half, :] + moved

    pl.when(has_down)(halo_up.wait_recv)
    fill_signal(2, halo[0])
    pl.when(has_up)(halo_down.wait_recv)
    fill_signal(0, halo[1])
    for k in range(1, per):
        gathers[k].wait_recv()
        fill_source(k)
    share(0)

    def shifted(count, first_row, group, h):
        def piece(b, hh):
            at = first_row + b * group
            return r32[at:at + count, hh * LANE:(hh + 1) * LANE]
        v = piece(1, h)
        if h > 0:
            v = v + piece(0, h - 1)
        if h < height - 1:
            v = v + piece(2, h + 1)
        return v

    r32[0:3 * channels, :] = jnp.dot(wb[...], xg[...], preferred_element_type=F32)
    spread(0)
    for h in range(height):
        part[pl.ds(h, channels, stride=height), :] = shifted(channels, 0, channels, h)

    sums = [send(rsend.at[k], rrecv.at[k], r_s.at[k], r_r.at[k], {"chan": flip(z, k)})
            for k in range(1, chan)]

    def block_of(t):
        return part[pl.ds(pl.multiple_of(t * rows, 16), rows), :]

    for k in range(1, chan):
        rsend[k] = block_of(flip(z, k)).astype(BF)

    for group in range(1, groups):
        for k in range(group * per, (group + 1) * per):
            gathers[k].wait_recv()
            if k == chan - 1:
                for c in sums:
                    c.start()
            fill_source(k)
        share(group)
        if group < groups - 1:
            spread(group)

    r32[0:9 * pad, :] = jnp.dot(wf[...], x3[:, LANE:LANE + span], preferred_element_type=F32)
    if groups > 1:
        spread(groups - 1)

    def relay(a):
        for h in range(height):
            t32[a, pl.ds(h, pad, stride=height), :] = shifted(pad, a * pad, 3 * pad, h)

    relay(0)
    psend[0] = t32[0, 0:rows, :].astype(BF)
    pair = (send(psend.at[0], precv.at[0], p_s.at[0], p_r.at[0], {"space": up}),
            send(psend.at[1], precv.at[1], p_s.at[1], p_r.at[1], {"space": down}))
    pl.when(has_up)(pair[0].start)
    relay(2)
    psend[1] = t32[2, 0:rows, :].astype(BF)
    pl.when(has_down)(pair[1].start)
    relay(1)

    for k in range(groups):
        collect(k)
    for a in range(3):
        for b in range(3):
            for c in range(3):
                at = (b * 3 + a) * some
                wg_ref[(a * 3 + b) * 3 + c] = (
                    acc[at:at + blk, c * wide:c * wide + channels] * scale)

    pl.when(has_down)(pair[0].wait_recv)
    pl.when(has_up)(pair[1].wait_recv)
    out_ref[...] = (t32[1, 0:rows, :] + precv[0].astype(F32)
                    + precv[1].astype(F32)).astype(BF)

    for c in sums:
        c.wait_recv()
    total = block_of(z)
    for k in range(1, chan):
        total = total + rrecv[k].astype(F32)
    back_ref[...] = total.astype(BF)

    for c in gathers[1:] + sums + pairs:
        c.wait_send()
    for group in shares:
        for c in group:
            c.wait_send()
    for c in (halo_up, pair[0]):
        pl.when(has_up)(c.wait_send)
    for c in (halo_down, pair[1]):
        pl.when(has_down)(c.wait_send)


def write(*refs):
    n = len(refs) // 2
    copies = [pltpu.make_async_copy(refs[i], refs[n + i], refs[-1].at[i]) for i in range(n)]
    for c in copies:
        c.start()
    for c in copies:
        c.wait()


def body(space, chan, activation, weights, cotangent):
    planes, blk, height, width = activation.shape
    channels = weights.shape[3]
    assert planes == 1 and width == LANE
    pad = up_to(blk, 16)
    rows = blk * height
    groups = min(chan, 4)
    scale = 1.0 / math.sqrt(planes * space * height * width)
    dma = pltpu.SemaphoreType.DMA
    vm = pltpu.VMEM
    deep = 3 * pad * chan
    gl = up_to(deep // groups, LANE)
    some = up_to(blk, 8)
    half = up_to(9 * some, 32) // 2
    wide = up_to(channels, LANE)
    shapes = (
        jax.ShapeDtypeStruct((rows, LANE), BF),
        jax.ShapeDtypeStruct((rows, LANE), BF),
        jax.ShapeDtypeStruct((27, blk, channels), F32),
    )
    outs = pl.pallas_call(
        functools.partial(kernel, space, chan, blk, pad, channels, height, groups, scale),
        out_shape=shapes,
        in_specs=[pl.BlockSpec(memory_space=pltpu.HBM)] * 3,
        out_specs=[pl.BlockSpec(memory_space=vm)] * 3,
        scratch_shapes=[
            vm((chan, rows, LANE), BF),
            vm((rows, LANE), BF),
            vm((27, channels, channels), BF),
            vm((deep, (height + 2) * LANE), BF),
            vm((9 * pad, height * LANE), BF),
            vm((3, 9 * pad, channels), BF),
            vm((9 * pad, deep), BF),
            vm((3 * channels, 9 * pad), BF),
            vm((3, pad * height, LANE), F32),
            vm((3, pad * height, LANE), F32),
            vm((max(9 * pad, 3 * channels), height * LANE), F32),
            vm((channels * height, LANE), F32),
            vm((2, rows, LANE), BF),
            vm((2, rows, LANE), BF),
            vm((2, rows, LANE), BF),
            vm((groups, 2 * half, gl), F32),
            vm((groups, half, gl), BF),
            vm((groups, half, gl), BF),
            vm((groups, space, half, gl), BF),
            vm((2 * half, 3 * wide), F32),
            vm((groups, gl, 3 * wide), BF),
            vm((chan, rows, LANE), BF),
            vm((chan, rows, LANE), BF),
            dma((3,)), dma((chan,)), dma((chan,)), dma((2,)), dma((2,)), dma((2,)), dma((2,)),
            dma((groups,)), dma((groups,)), dma((groups, space)), dma((groups, space)),
            dma((chan,)), dma((chan,)),
        ],
        compiler_params=pltpu.CompilerParams(
            collective_id=0, has_side_effects=True, vmem_limit_bytes=40 * 2**20),
    )(*[pltpu.with_memory_space_constraint(x, pltpu.HBM) for x in (
        activation.reshape(rows, width), cotangent.reshape(rows, width),
        weights.reshape(27, channels, channels))])
    out, back, grads = pl.pallas_call(
        write,
        out_shape=shapes,
        in_specs=[pl.BlockSpec(memory_space=vm)] * 3,
        out_specs=[pl.BlockSpec(memory_space=pltpu.HBM)] * 3,
        scratch_shapes=[dma((3,))],
        compiler_params=pltpu.CompilerParams(vmem_limit_bytes=2**20),
    )(*outs)
    field = (1, blk, height, width)
    grads = jnp.swapaxes(grads.reshape(3, 3, 3, blk, channels), 3, 4)
    return out.reshape(field), back.reshape(field), grads


def solution(mesh):
    field = P("space", "chan", None, None)
    return jax.shard_map(
        functools.partial(body, mesh.shape["space"], mesh.shape["chan"]),
        mesh=mesh,
        in_specs=(field, P(), field),
        out_specs=(field, field, P(None, None, None, None, "chan")),
        check_vma=False,
    )
```

time: 31.5 us -> 28 us (0.89)
  local copies, waits for them, and re-layouts: 4.88 us -> 0 us
  Pallas kernels: 25.8 us -> 27.2 us
    unnamed x9 -> x0, local copies, waits for them, and re-layouts: 4.88 us -> none
    pallas_call x0 -> x1, Pallas kernels: none -> 0.82 us  [body(): pl.pallas_call(write, out_shape=shapes, in_specs=[pl.BlockSpec(memory_spa...]
    pallas_call x1, Pallas kernels: 25.8 us -> 26.4 us  [body(): pl.pallas_call(functools.partial(kernel, space, chan, blk, pad, channels,...]
where the time goes in v1:
time: 28 us; the launch traced here: 27.8 us
  Pallas kernels  27.2 us (97%)
  between operations  0.64 us (2%)
    pallas_call x1, Pallas kernels, body(): pl.pallas_call(functools.partial(kernel, space, chan, blk, pad, channels,...  26.4 us
    pallas_call x1, Pallas kernels, body(): pl.pallas_call(write, out_shape=shapes, in_specs=[pl.BlockSpec(memory_spa...  0.82 us

profile of v1, /device:TPU:0, one launch (start us, length us, event | category | flops | bytes accessed | tf_op | source)
XLA Modules:
  0.0 27.8 jit_solution(6493362330131272549)
XLA Ops:
  0.6 26.4 %shard_map.58 = (bf16[384,128]{1,0:T(8,128)(2,1)S(1)}, bf16[384,128]{1,0:T(8,128)(2,1)S(1)}, f32[27,24,96]{2,1,0:T(8,128)S(1)}) custom-call(bf16[384,128]{1,0:T(8,128)(2,1)} %bitcast.9, bf16[384,128]{1,0:T(8,128)(2,1)} %bitcast.10, bf16[27,96,96]{2,1,0:T(8,128)(2,1)} %bitcast.8), custom_call_target="tpu_custom_call" | custom-call | tf_op jit(solution)/shard_map/pallas_call | solution.py:324
  27.0 0.8 %shard_map.59 = (bf16[384,128]{1,0:T(8,128)(2,1)}, bf16[384,128]{1,0:T(8,128)(2,1)}, f32[27,24,96]{2,1,0:T(8,128)}) custom-call(bf16[384,128]{1,0:T(8,128)(2,1)S(1)} %get-tuple-element.9.refs_0_, bf16[384,128]{1,0:T(8,128)(2,1)S(1)} %get-tuple-element.10.refs_1_, f32[27,24,96]{2,1,0:T(8,128)S(1)} %get-tuple-element.11.refs_2_), custom_call_target="tpu_custom_call" | custom-call | tf_op jit(solution)/shard_map/pallas_call | solution.py:362

commit v2 on v1

--- a/solution.py
+++ b/solution.py
@@ -29,16 +29,18 @@
 def kernel(space, chan, blk, pad, channels, height, groups, scale,
            a_hbm, g_hbm, w_hbm, out_ref, back_ref, wg_ref,
            ga, gv, w_ref, x3, xg, wt, wf, wb, z32, t32, r32, part,
-           halo, psend, precv, wflat, csend, crecv, wall, acc, place_q,
+           halo, psend, precv, wflat, csend, crecv, wall, full, stack, acc, place_q,
            rsend, rrecv,
-           l_s, g_s, g_r, h_s, h_r, p_s, p_r, c_s, c_r, w_s, w_r, r_s, r_r):
+           l_s, g_s, g_r, h_s, h_r, p_s, p_r, c_s, c_r, w_s, w_r, f_s, f_r, r_s, r_r):
     e = lax.axis_index("space")
     z = lax.axis_index("chan")
     rows = blk * height
     span = height * LANE
     per = chan // groups
-    half, gl = wall.shape[2], wall.shape[3]
-    some = -(-blk // 8) * 8
+    tall, half = wall.shape[2], wall.shape[3]
+    some = up_to(blk, 8)
+    ring = up_to(3 * some, 16)
+    each = 3 * some if per == 1 else per * ring
     wide = acc.shape[1] // 3
     up, down = lax.rem(e + 1, space), lax.rem(e + space - 1, space)
     core = lax.rem(e, 2)
@@ -87,22 +89,27 @@
     wflat[...] = jnp.zeros_like(wflat)
     few = lax.broadcasted_iota(jnp.int32, (rows, LANE), 1)
 
-    def fill(dst, row_of, first, src):
+    def shift(src):
         v = src.astype(F32)
         z32[0, 0:rows, :] = jnp.where(few == 0, 0.0, pltpu.roll(v, 1, 1))
         z32[1, 0:rows, :] = v
         z32[2, 0:rows, :] = jnp.where(few == LANE - 1, 0.0, pltpu.roll(v, LANE - 1, 1))
+
+    def fill_signal(a, src):
+        shift(src)
         for c in range(3):
-            at = row_of(c)
+            at = (c * 3 + a) * pad
             for h in range(height):
-                dst[at:at + pad, (h + first) * LANE:(h + first + 1) * LANE] = (
+                xg[at:at + pad, h * LANE:(h + 1) * LANE] = (
                     z32[c, pl.ds(h, pad, stride=height), :].astype(BF))
 
-    def fill_signal(a, src):
-        fill(xg, lambda c: (c * 3 + a) * pad, 0, src)
-
     def fill_source(k):
-        fill(x3, lambda c: (k * 3 + c) * pad, 1, ga[k])
+        shift(ga[k])
+        rest = [jnp.zeros((ring - 3 * some, LANE), F32)] if ring > 3 * some else []
+        for h in range(height):
+            taps = [z32[c, pl.ds(h, some, stride=height), :] for c in range(3)]
+            x3[k * ring:(k + 1) * ring, (h + 1) * LANE:(h + 2) * LANE] = (
+                jnp.concatenate(taps + rest, axis=0).astype(BF))
 
     loads[0].wait()
     fill_signal(1, gv[...])
@@ -134,49 +141,53 @@
                 wt[c, at:at + pad, :] = lax.dot_general(
                     pick, w_ref[(a * 3 + b) * 3 + c], ROWS_T,
                     preferred_element_type=F32).astype(BF)
-    deep = 3 * pad * chan
+    deep = x3.shape[0]
     channel = lax.broadcasted_iota(jnp.int32, (channels, deep), 0)
     spot = lax.broadcasted_iota(jnp.int32, (channels, deep), 1)
     goes = jnp.zeros((channels, deep), jnp.int32)
     for k in range(chan):
         local = channel - flip(z, k) * blk
-        goes = jnp.where((local >= 0) & (local < blk), local + k * 3 * pad, goes)
+        goes = jnp.where((local >= 0) & (local < blk), local + k * ring, goes)
     total = jnp.zeros((9 * pad, deep), F32)
     for c in range(3):
         total = total + jnp.dot(
-            wt[c], jnp.where(spot == goes + c * pad, 1.0, 0.0).astype(BF),
+            wt[c], jnp.where(spot == goes + c * some, 1.0, 0.0).astype(BF),
             preferred_element_type=F32)
     wf[...] = total.astype(BF)
 
     place_q[...] = jnp.zeros_like(place_q)
-    row = lax.broadcasted_iota(jnp.int32, (pad, wide), 0)
-    col = lax.broadcasted_iota(jnp.int32, (pad, wide), 1)
+    row = lax.broadcasted_iota(jnp.int32, (ring, wide), 0)
+    col = lax.broadcasted_iota(jnp.int32, (ring, wide), 1)
     for k in range(chan):
-        hit = (row < blk) & (col == row + flip(z, k) * blk)
-        block = jnp.where(hit, 1.0, 0.0).astype(BF)
+        at = (k % per) * ring
         for c in range(3):
-            at = ((k % per) * 3 + c) * pad
-            place_q[k // per, at:at + pad, c * wide:(c + 1) * wide] = block
+            own = row - c * some
+            hit = (own >= 0) & (own < blk) & (col == own + flip(z, k) * blk)
+            place_q[k // per, at:at + ring, c * wide:(c + 1) * wide] = (
+                jnp.where(hit, 1.0, 0.0).astype(BF))
 
     pairs = [send(csend.at[k], crecv.at[k], c_s.at[k], c_r.at[k], {"space": flip(e, 1)})
              for k in range(groups)]
     shares = [[send(wall.at[k, e], wall.at[k, e], w_s.at[k, m], w_r.at[k, m],
-                    {"space": flip(e, m)}) for m in range(1, space)]
+                    {"space": flip(e, m)})
+               for m in range(1 if k == groups - 1 else 2, space, 1 if k == groups - 1 else 2)]
               for k in range(groups)]
+    passes = [send(full.at[k, core], full.at[k, core], f_s.at[k], f_r.at[k],
+                   {"space": flip(e, 1)}) for k in range(groups - 1)]
 
     def my_half(k, which):
-        return wflat[k, pl.ds(pl.multiple_of(which * half, 16), half), :]
+        return wflat[k, :, pl.ds(pl.multiple_of(which * half, LANE), half)]
 
     def share(k):
-        many = per * 3 * pad
+        many = per * ring
         for b in range(3):
             one = lax.dot_general(
                 xg[3 * pad:6 * pad, :],
                 x3[k * many:(k + 1) * many, b * LANE:b * LANE + span],
                 ROWS_T, preferred_element_type=F32)
             for a in range(3):
-                at = (b * 3 + a) * some
-                wflat[k, at:at + some, 0:many] = one[a * pad:a * pad + some, :]
+                wflat[k, a * some:(a + 1) * some, b * each:(b + 1) * each] = (
+                    one[a * pad:a * pad + some, 0:each])
         csend[k] = my_half(k, 1 - core).astype(BF)
         pairs[k].start()
 
@@ -186,16 +197,30 @@
         for c in shares[k]:
             c.start()
 
-    def collect(k):
+    def summed(k, side):
+        total = wall[k, side].astype(F32)
+        for chip in range(1, space // 2):
+            total = total + wall[k, 2 * chip + side].astype(F32)
+        return total.astype(BF)
+
+    def gather_up(k):
         for c in shares[k]:
             c.wait_recv()
-        for side in range(2):
-            total = wall[k, side].astype(F32)
-            for chip in range(1, space // 2):
-                total = total + wall[k, 2 * chip + side].astype(F32)
-            moved = jnp.dot(total.astype(BF), place_q[k], preferred_element_type=F32)
-            at = side * half
-            acc[at:at + half, :] = moved if k == 0 else acc[at:at + half, :] + moved
+        if k == groups - 1:
+            for side in range(2):
+                full[k, side] = summed(k, side)
+        else:
+            full[k, core] = summed(k, core)
+            passes[k].start()
+
+    def collect(k):
+        if k < groups - 1:
+            passes[k].wait_recv()
+        both = jnp.concatenate([full[k, 0], full[k, 1]], axis=1)
+        for b in range(3):
+            stack[b * tall:(b + 1) * tall, 0:each] = both[:, b * each:(b + 1) * each]
+        moved = jnp.dot(stack[...], place_q[k], preferred_element_type=F32)
+        acc[...] = moved if k == 0 else acc[...] + moved
 
     pl.when(has_down)(halo_up.wait_recv)
     fill_signal(2, halo[0])
@@ -234,13 +259,15 @@
     for group in range(1, groups):
         for k in range(group * per, (group + 1) * per):
             gathers[k].wait_recv()
-            if k == chan - 1:
+            if k == chan - 2:
                 for c in sums:
                     c.start()
             fill_source(k)
         share(group)
         if group < groups - 1:
             spread(group)
+    if groups > 1:
+        gather_up(0)
 
     r32[0:9 * pad, :] = jnp.dot(wf[...], x3[:, LANE:LANE + span], preferred_element_type=F32)
     if groups > 1:
@@ -250,6 +277,7 @@
         for h in range(height):
             t32[a, pl.ds(h, pad, stride=height), :] = shifted(pad, a * pad, 3 * pad, h)
 
+    stack[...] = jnp.zeros_like(stack)
     relay(0)
     psend[0] = t32[0, 0:rows, :].astype(BF)
     pair = (send(psend.at[0], precv.at[0], p_s.at[0], p_r.at[0], {"space": up}),
@@ -258,14 +286,18 @@
     relay(2)
     psend[1] = t32[2, 0:rows, :].astype(BF)
     pl.when(has_down)(pair[1].start)
+    for k in range(1, groups - 1):
+        gather_up(k)
     relay(1)
 
-    for k in range(groups):
+    for k in range(groups - 1):
         collect(k)
+    gather_up(groups - 1)
+    collect(groups - 1)
     for a in range(3):
         for b in range(3):
             for c in range(3):
-                at = (b * 3 + a) * some
+                at = b * tall + a * some
                 wg_ref[(a * 3 + b) * 3 + c] = (
                     acc[at:at + blk, c * wide:c * wide + channels] * scale)
 
@@ -281,7 +313,7 @@
         total = total + rrecv[k].astype(F32)
     back_ref[...] = total.astype(BF)
 
-    for c in gathers[1:] + sums + pairs:
+    for c in gathers[1:] + sums + pairs + passes:
         c.wait_send()
     for group in shares:
         for c in group:
@@ -311,10 +343,13 @@
     scale = 1.0 / math.sqrt(planes * space * height * width)
     dma = pltpu.SemaphoreType.DMA
     vm = pltpu.VMEM
-    deep = 3 * pad * chan
-    gl = up_to(deep // groups, LANE)
     some = up_to(blk, 8)
-    half = up_to(9 * some, 32) // 2
+    ring = up_to(3 * some, 16)
+    deep = ring * chan
+    per = chan // groups
+    tall = ring
+    half = up_to(3 * (3 * some if per == 1 else per * ring), 2 * LANE) // 2
+    flat = up_to(per * ring, LANE)
     wide = up_to(channels, LANE)
     shapes = (
         jax.ShapeDtypeStruct((rows, LANE), BF),
@@ -342,16 +377,19 @@
             vm((2, rows, LANE), BF),
             vm((2, rows, LANE), BF),
             vm((2, rows, LANE), BF),
-            vm((groups, 2 * half, gl), F32),
-            vm((groups, half, gl), BF),
-            vm((groups, half, gl), BF),
-            vm((groups, space, half, gl), BF),
-            vm((2 * half, 3 * wide), F32),
-            vm((groups, gl, 3 * wide), BF),
+            vm((groups, tall, 2 * half), F32),
+            vm((groups, tall, half), BF),
+            vm((groups, tall, half), BF),
+            vm((groups, space, tall, half), BF),
+            vm((groups, 2, tall, half), BF),
+            vm((3 * tall, flat), BF),
+            vm((3 * tall, 3 * wide), F32),
+            vm((groups, flat, 3 * wide), BF),
             vm((chan, rows, LANE), BF),
             vm((chan, rows, LANE), BF),
             dma((3,)), dma((chan,)), dma((chan,)), dma((2,)), dma((2,)), dma((2,)), dma((2,)),
             dma((groups,)), dma((groups,)), dma((groups, space)), dma((groups, space)),
+            dma((groups,)), dma((groups,)),
             dma((chan,)), dma((chan,)),
         ],
         compiler_params=pltpu.CompilerParams(

time: 28 us -> 26 us (0.929)
  Pallas kernels: 27.2 us -> 25.2 us
    pallas_call x1, Pallas kernels: 26.4 us -> 24.4 us  [body(): pl.pallas_call(functools.partial(kernel, space, chan, blk, pad, channels,...]
where the time goes in v2:
time: 26 us; the launch traced here: 25.8 us
  Pallas kernels  25.2 us (97%)
  between operations  0.64 us (2%)
    pallas_call x1, Pallas kernels, body(): pl.pallas_call(functools.partial(kernel, space, chan, blk, pad, channels,...  24.4 us
    pallas_call x1, Pallas kernels, body(): pl.pallas_call(write, out_shape=shapes, in_specs=[pl.BlockSpec(memory_spa...  0.82 us

profile of v2, /device:TPU:0, one launch (start us, length us, event | category | flops | bytes accessed | tf_op | source)
XLA Modules:
  0.0 25.8 jit_solution(8086629478611227530)
XLA Ops:
  0.6 24.4 %shard_map.58 = (bf16[384,128]{1,0:T(8,128)(2,1)S(1)}, bf16[384,128]{1,0:T(8,128)(2,1)S(1)}, f32[27,24,96]{2,1,0:T(8,128)S(1)}) custom-call(bf16[384,128]{1,0:T(8,128)(2,1)} %bitcast.9, bf16[384,128]{1,0:T(8,128)(2,1)} %bitcast.10, bf16[27,96,96]{2,1,0:T(8,128)(2,1)} %bitcast.8), custom_call_target="tpu_custom_call" | custom-call | tf_op jit(solution)/shard_map/pallas_call | solution.py:359
  25.0 0.8 %shard_map.59 = (bf16[384,128]{1,0:T(8,128)(2,1)}, bf16[384,128]{1,0:T(8,128)(2,1)}, f32[27,24,96]{2,1,0:T(8,128)}) custom-call(bf16[384,128]{1,0:T(8,128)(2,1)S(1)} %get-tuple-element.9.refs_0_, bf16[384,128]{1,0:T(8,128)(2,1)S(1)} %get-tuple-element.10.refs_1_, f32[27,24,96]{2,1,0:T(8,128)S(1)} %get-tuple-element.11.refs_2_), custom_call_target="tpu_custom_call" | custom-call | tf_op jit(solution)/shard_map/pallas_call | solution.py:400

commit v3 on v2

--- a/solution.py
+++ b/solution.py
@@ -30,8 +30,8 @@
            a_hbm, g_hbm, w_hbm, out_ref, back_ref, wg_ref,
            ga, gv, w_ref, x3, xg, wt, wf, wb, z32, t32, r32, part,
            halo, psend, precv, wflat, csend, crecv, wall, full, stack, acc, place_q,
-           rsend, rrecv,
-           l_s, g_s, g_r, h_s, h_r, p_s, p_r, c_s, c_r, w_s, w_r, f_s, f_r, r_s, r_r):
+           nsend, nrecv, rsend, rrecv,
+           l_s, g_s, g_r, h_s, h_r, p_s, p_r, c_s, c_r, w_s, w_r, f_s, f_r, n_s, n_r, r_s, r_r):
     e = lax.axis_index("space")
     z = lax.axis_index("chan")
     rows = blk * height
@@ -50,8 +50,8 @@
     others += [{"space": flip(e, k)} for k in range(1, space)]
     for other in others:
         pl.semaphore_signal(barrier, inc=1, device_id=other)
-    loads = [pltpu.make_async_copy(g_hbm, gv, l_s.at[0]),
-             pltpu.make_async_copy(a_hbm, ga.at[0], l_s.at[1]),
+    loads = [pltpu.make_async_copy(a_hbm, ga.at[0], l_s.at[1]),
+             pltpu.make_async_copy(g_hbm, gv, l_s.at[0]),
              pltpu.make_async_copy(w_hbm, w_ref, l_s.at[2])]
     for c in loads:
         c.start()
@@ -60,15 +60,17 @@
         return pltpu.make_async_remote_copy(src, dst, ssem, rsem, device_id=to)
 
     gathers = [None] + [
-        send(a_hbm, ga.at[k], g_s.at[k], g_r.at[k], {"chan": flip(z, k)})
+        send(ga.at[0], ga.at[k], g_s.at[k], g_r.at[k], {"chan": flip(z, k)})
         for k in range(1, chan)]
-    halo_up = send(g_hbm, halo.at[0], h_s.at[0], h_r.at[0], {"space": up})
-    halo_down = send(g_hbm, halo.at[1], h_s.at[1], h_r.at[1], {"space": down})
+    halo_up = send(gv, halo.at[0], h_s.at[0], h_r.at[0], {"space": up})
+    halo_down = send(gv, halo.at[1], h_s.at[1], h_r.at[1], {"space": down})
     has_up, has_down = e < space - 1, e > 0
 
     pl.semaphore_wait(barrier, len(others))
+    loads[0].wait()
     for c in gathers[1:]:
         c.start()
+    loads[1].wait()
     pl.when(has_up)(halo_up.start)
     pl.when(has_down)(halo_down.start)
 
@@ -87,6 +89,7 @@
     x3[:, 0:LANE] = jnp.zeros((x3.shape[0], LANE), BF)
     x3[:, span + LANE:span + 2 * LANE] = jnp.zeros((x3.shape[0], LANE), BF)
     wflat[...] = jnp.zeros_like(wflat)
+    stack[...] = jnp.zeros_like(stack)
     few = lax.broadcasted_iota(jnp.int32, (rows, LANE), 1)
 
     def shift(src):
@@ -111,9 +114,7 @@
             x3[k * ring:(k + 1) * ring, (h + 1) * LANE:(h + 2) * LANE] = (
                 jnp.concatenate(taps + rest, axis=0).astype(BF))
 
-    loads[0].wait()
     fill_signal(1, gv[...])
-    loads[1].wait()
     fill_source(0)
 
     loads[2].wait()
@@ -170,10 +171,10 @@
              for k in range(groups)]
     shares = [[send(wall.at[k, e], wall.at[k, e], w_s.at[k, m], w_r.at[k, m],
                     {"space": flip(e, m)})
-               for m in range(1 if k == groups - 1 else 2, space, 1 if k == groups - 1 else 2)]
+               for m in reversed(range(2, space, 2))]
               for k in range(groups)]
     passes = [send(full.at[k, core], full.at[k, core], f_s.at[k], f_r.at[k],
-                   {"space": flip(e, 1)}) for k in range(groups - 1)]
+                   {"space": flip(e, 1)}) for k in range(groups)]
 
     def my_half(k, which):
         return wflat[k, :, pl.ds(pl.multiple_of(which * half, LANE), half)]
@@ -206,16 +207,11 @@
     def gather_up(k):
         for c in shares[k]:
             c.wait_recv()
-        if k == groups - 1:
-            for side in range(2):
-                full[k, side] = summed(k, side)
-        else:
-            full[k, core] = summed(k, core)
-            passes[k].start()
+        full[k, core] = summed(k, core)
+        passes[k].start()
 
     def collect(k):
-        if k < groups - 1:
-            passes[k].wait_recv()
+        passes[k].wait_recv()
         both = jnp.concatenate([full[k, 0], full[k, 1]], axis=1)
         for b in range(3):
             stack[b * tall:(b + 1) * tall, 0:each] = both[:, b * each:(b + 1) * each]
@@ -247,37 +243,46 @@
     for h in range(height):
         part[pl.ds(h, channels, stride=height), :] = shifted(channels, 0, channels, h)
 
-    sums = [send(rsend.at[k], rrecv.at[k], r_s.at[k], r_r.at[k], {"chan": flip(z, k)})
-            for k in range(1, chan)]
+    near = [send(nsend.at[k], nrecv.at[k], n_s.at[k], n_r.at[k], {"chan": flip(z, 1)})
+            for k in range(chan // 2)]
+    sums = [send(rsend.at[k], rrecv.at[k], r_s.at[k], r_r.at[k], {"chan": flip(z, 2 * k)})
+            for k in range(1, chan // 2)]
 
     def block_of(t):
         return part[pl.ds(pl.multiple_of(t * rows, 16), rows), :]
 
-    for k in range(1, chan):
-        rsend[k] = block_of(flip(z, k)).astype(BF)
+    for k in reversed(range(chan // 2)):
+        nsend[k] = block_of(flip(z, 2 * k + 1)).astype(BF)
+    for c in near[1:]:
+        c.start()
+
+    def pass_on():
+        for k in range(1, chan // 2):
+            near[k].wait_recv()
+            rsend[k] = (block_of(flip(z, 2 * k)) + nrecv[k].astype(F32)).astype(BF)
+            sums[k - 1].start()
 
     for group in range(1, groups):
         for k in range(group * per, (group + 1) * per):
             gathers[k].wait_recv()
-            if k == chan - 2:
-                for c in sums:
-                    c.start()
+            if k == chan - 1:
+                near[0].start()
             fill_source(k)
         share(group)
-        if group < groups - 1:
-            spread(group)
-    if groups > 1:
-        gather_up(0)
-
-    r32[0:9 * pad, :] = jnp.dot(wf[...], x3[:, LANE:LANE + span], preferred_element_type=F32)
+        if group == 1 and groups > 2:
+            spread(1)
+        elif group > 2:
+            spread(group - 1)
+
+    pass_on()
     if groups > 1:
         spread(groups - 1)
+    r32[0:9 * pad, :] = jnp.dot(wf[...], x3[:, LANE:LANE + span], preferred_element_type=F32)
 
     def relay(a):
         for h in range(height):
             t32[a, pl.ds(h, pad, stride=height), :] = shifted(pad, a * pad, 3 * pad, h)
 
-    stack[...] = jnp.zeros_like(stack)
     relay(0)
     psend[0] = t32[0, 0:rows, :].astype(BF)
     pair = (send(psend.at[0], precv.at[0], p_s.at[0], p_r.at[0], {"space": up}),
@@ -286,7 +291,7 @@
     relay(2)
     psend[1] = t32[2, 0:rows, :].astype(BF)
     pl.when(has_down)(pair[1].start)
-    for k in range(1, groups - 1):
+    for k in range(groups - 1):
         gather_up(k)
     relay(1)
 
@@ -308,12 +313,13 @@
 
     for c in sums:
         c.wait_recv()
-    total = block_of(z)
-    for k in range(1, chan):
+    near[0].wait_recv()
+    total = block_of(z) + nrecv[0].astype(F32)
+    for k in range(1, chan // 2):
         total = total + rrecv[k].astype(F32)
     back_ref[...] = total.astype(BF)
 
-    for c in gathers[1:] + sums + pairs + passes:
+    for c in gathers[1:] + near + sums + pairs + passes:
         c.wait_send()
     for group in shares:
         for c in group:
@@ -385,12 +391,14 @@
             vm((3 * tall, flat), BF),
             vm((3 * tall, 3 * wide), F32),
             vm((groups, flat, 3 * wide), BF),
-            vm((chan, rows, LANE), BF),
-            vm((chan, rows, LANE), BF),
+            vm((chan // 2, rows, LANE), BF),
+            vm((chan // 2, rows, LANE), BF),
+            vm((chan // 2, rows, LANE), BF),
+            vm((chan // 2, rows, LANE), BF),
             dma((3,)), dma((chan,)), dma((chan,)), dma((2,)), dma((2,)), dma((2,)), dma((2,)),
             dma((groups,)), dma((groups,)), dma((groups, space)), dma((groups, space)),
             dma((groups,)), dma((groups,)),
-            dma((chan,)), dma((chan,)),
+            dma((chan // 2,)), dma((chan // 2,)), dma((chan // 2,)), dma((chan // 2,)),
         ],
         compiler_params=pltpu.CompilerParams(
             collective_id=0, has_side_effects=True, vmem_limit_bytes=40 * 2**20),

time: 26 us -> 25 us (0.962)
  Pallas kernels: 25.2 us -> 24.2 us
    pallas_call x1, Pallas kernels: 24.4 us -> 23.4 us  [body(): pl.pallas_call(functools.partial(kernel, space, chan, blk, pad, channels,...]
where the time goes in v3:
time: 25 us; the launch traced here: 24.9 us
  Pallas kernels  24.2 us (97%)
  between operations  0.64 us (3%)
    pallas_call x1, Pallas kernels, body(): pl.pallas_call(functools.partial(kernel, space, chan, blk, pad, channels,...  23.4 us
    pallas_call x1, Pallas kernels, body(): pl.pallas_call(write, out_shape=shapes, in_specs=[pl.BlockSpec(memory_spa...  0.82 us

profile of v3, /device:TPU:0, one launch (start us, length us, event | category | flops | bytes accessed | tf_op | source)
XLA Modules:
  0.0 24.9 jit_solution(9168071670779569495)
XLA Ops:
  0.6 23.4 %shard_map.58 = (bf16[384,128]{1,0:T(8,128)(2,1)S(1)}, bf16[384,128]{1,0:T(8,128)(2,1)S(1)}, f32[27,24,96]{2,1,0:T(8,128)S(1)}) custom-call(bf16[384,128]{1,0:T(8,128)(2,1)} %bitcast.9, bf16[384,128]{1,0:T(8,128)(2,1)} %bitcast.10, bf16[27,96,96]{2,1,0:T(8,128)(2,1)} %bitcast.8), custom_call_target="tpu_custom_call" | custom-call | tf_op jit(solution)/shard_map/pallas_call | solution.py:365
  24.0 0.8 %shard_map.59 = (bf16[384,128]{1,0:T(8,128)(2,1)}, bf16[384,128]{1,0:T(8,128)(2,1)}, f32[27,24,96]{2,1,0:T(8,128)}) custom-call(bf16[384,128]{1,0:T(8,128)(2,1)S(1)} %get-tuple-element.9.refs_0_, bf16[384,128]{1,0:T(8,128)(2,1)S(1)} %get-tuple-element.10.refs_1_, f32[27,24,96]{2,1,0:T(8,128)S(1)} %get-tuple-element.11.refs_2_), custom_call_target="tpu_custom_call" | custom-call | tf_op jit(solution)/shard_map/pallas_call | solution.py:408

commit v4 on v3

--- a/solution.py
+++ b/solution.py
@@ -26,7 +26,7 @@
     return out
 
 
-def kernel(space, chan, blk, pad, channels, height, groups, scale,
+def kernel(space, chan, blk, pad, channels, height, cuts, scale,
            a_hbm, g_hbm, w_hbm, out_ref, back_ref, wg_ref,
            ga, gv, w_ref, x3, xg, wt, wf, wb, z32, t32, r32, part,
            halo, psend, precv, wflat, csend, crecv, wall, full, stack, acc, place_q,
@@ -36,11 +36,12 @@
     z = lax.axis_index("chan")
     rows = blk * height
     span = height * LANE
-    per = chan // groups
-    tall, half = wall.shape[2], wall.shape[3]
+    groups = len(cuts)
+    begin = [sum(cuts[:g]) for g in range(groups + 1)]
+    tall = full[0].shape[1]
     some = up_to(blk, 8)
     ring = up_to(3 * some, 16)
-    each = 3 * some if per == 1 else per * ring
+    each = [n * ring for n in cuts]
     wide = acc.shape[1] // 3
     up, down = lax.rem(e + 1, space), lax.rem(e + space - 1, space)
     core = lax.rem(e, 2)
@@ -88,8 +89,8 @@
     z32[...] = jnp.zeros_like(z32)
     x3[:, 0:LANE] = jnp.zeros((x3.shape[0], LANE), BF)
     x3[:, span + LANE:span + 2 * LANE] = jnp.zeros((x3.shape[0], LANE), BF)
-    wflat[...] = jnp.zeros_like(wflat)
-    stack[...] = jnp.zeros_like(stack)
+    for ref in (*wflat, *stack, *place_q):
+        ref[...] = jnp.zeros_like(ref)
     few = lax.broadcasted_iota(jnp.int32, (rows, LANE), 1)
 
     def shift(src):
@@ -156,76 +157,88 @@
             preferred_element_type=F32)
     wf[...] = total.astype(BF)
 
-    place_q[...] = jnp.zeros_like(place_q)
     row = lax.broadcasted_iota(jnp.int32, (ring, wide), 0)
     col = lax.broadcasted_iota(jnp.int32, (ring, wide), 1)
-    for k in range(chan):
-        at = (k % per) * ring
-        for c in range(3):
-            own = row - c * some
-            hit = (own >= 0) & (own < blk) & (col == own + flip(z, k) * blk)
-            place_q[k // per, at:at + ring, c * wide:(c + 1) * wide] = (
-                jnp.where(hit, 1.0, 0.0).astype(BF))
-
-    pairs = [send(csend.at[k], crecv.at[k], c_s.at[k], c_r.at[k], {"space": flip(e, 1)})
-             for k in range(groups)]
-    shares = [[send(wall.at[k, e], wall.at[k, e], w_s.at[k, m], w_r.at[k, m],
-                    {"space": flip(e, m)})
-               for m in reversed(range(2, space, 2))]
-              for k in range(groups)]
-    passes = [send(full.at[k, core], full.at[k, core], f_s.at[k], f_r.at[k],
-                   {"space": flip(e, 1)}) for k in range(groups)]
-
-    def my_half(k, which):
-        return wflat[k, :, pl.ds(pl.multiple_of(which * half, LANE), half)]
-
-    def share(k):
-        many = per * ring
+    for g in range(groups):
+        for k in range(begin[g], begin[g + 1]):
+            at = (k - begin[g]) * ring
+            for c in range(3):
+                own = row - c * some
+                hit = (own >= 0) & (own < blk) & (col == own + flip(z, k) * blk)
+                place_q[g][at:at + ring, c * wide:(c + 1) * wide] = (
+                    jnp.where(hit, 1.0, 0.0).astype(BF))
+
+    last = groups - 1
+    pairs = [send(csend[g], crecv[g], c_s.at[g], c_r.at[g], {"space": flip(e, 1)})
+             for g in range(last)]
+
+    def reach(g):
+        return range(1 if g == last else 2, space, 1 if g == last else 2)
+
+    def piece_of(g, m):
+        return csend[g] if m % 2 else wall[g].at[e]
+
+    shares = [[send(piece_of(g, m), wall[g].at[e], w_s.at[g, m], w_r.at[g, m],
+                    {"space": flip(e, m)}) for m in reversed(reach(g))]
+              for g in range(groups)]
+    passes = [send(full[g].at[core], full[g].at[core], f_s.at[g], f_r.at[g],
+                   {"space": flip(e, 1)}) for g in range(groups)]
+
+    def my_half(g, which):
+        half = full[g].shape[2]
+        return wflat[g][:, pl.ds(pl.multiple_of(which * half, LANE), half)]
+
+    def share(g):
         for b in range(3):
             one = lax.dot_general(
                 xg[3 * pad:6 * pad, :],
-                x3[k * many:(k + 1) * many, b * LANE:b * LANE + span],
+                x3[begin[g] * ring:begin[g + 1] * ring, b * LANE:b * LANE + span],
                 ROWS_T, preferred_element_type=F32)
             for a in range(3):
-                wflat[k, a * some:(a + 1) * some, b * each:(b + 1) * each] = (
-                    one[a * pad:a * pad + some, 0:each])
-        csend[k] = my_half(k, 1 - core).astype(BF)
-        pairs[k].start()
-
-    def spread(k):
-        pairs[k].wait_recv()
-        wall[k, e] = (my_half(k, core) + crecv[k].astype(F32)).astype(BF)
-        for c in shares[k]:
+                wflat[g][a * some:(a + 1) * some, b * each[g]:(b + 1) * each[g]] = (
+                    one[a * pad:a * pad + some, :])
+        csend[g][...] = my_half(g, 1 - core).astype(BF)
+        if g == last:
+            wall[g][e] = my_half(g, core).astype(BF)
+            for c in shares[g]:
+                c.start()
+        else:
+            pairs[g].start()
+
+    def spread(g):
+        if g == last:
+            return
+        pairs[g].wait_recv()
+        wall[g][e] = (my_half(g, core) + crecv[g][...].astype(F32)).astype(BF)
+        for c in shares[g]:
             c.start()
 
-    def summed(k, side):
-        total = wall[k, side].astype(F32)
-        for chip in range(1, space // 2):
-            total = total + wall[k, 2 * chip + side].astype(F32)
-        return total.astype(BF)
-
-    def gather_up(k):
-        for c in shares[k]:
+    def gather_up(g):
+        for c in shares[g]:
             c.wait_recv()
-        full[k, core] = summed(k, core)
-        passes[k].start()
-
-    def collect(k):
-        passes[k].wait_recv()
-        both = jnp.concatenate([full[k, 0], full[k, 1]], axis=1)
+        if g == last:
+            total = wall[g][0].astype(F32)
+            for origin in range(1, space):
+                total = total + wall[g][origin].astype(F32)
+        else:
+            total = wall[g][core].astype(F32)
+            for chip in range(1, space // 2):
+                total = total + wall[g][2 * chip + core].astype(F32)
+        full[g][core] = total.astype(BF)
+        passes[g].start()
+
+    def collect(g):
+        passes[g].wait_recv()
+        both = jnp.concatenate([full[g][0], full[g][1]], axis=1)
         for b in range(3):
-            stack[b * tall:(b + 1) * tall, 0:each] = both[:, b * each:(b + 1) * each]
-        moved = jnp.dot(stack[...], place_q[k], preferred_element_type=F32)
-        acc[...] = moved if k == 0 else acc[...] + moved
+            stack[g][b * tall:(b + 1) * tall, 0:each[g]] = both[:, b * each[g]:(b + 1) * each[g]]
+        moved = jnp.dot(stack[g][...], place_q[g][...], preferred_element_type=F32)
+        acc[...] = moved if g == 0 else acc[...] + moved
 
     pl.when(has_down)(halo_up.wait_recv)
     fill_signal(2, halo[0])
     pl.when(has_up)(halo_down.wait_recv)
     fill_signal(0, halo[1])
-    for k in range(1, per):
-        gathers[k].wait_recv()
-        fill_source(k)
-    share(0)
 
     def shifted(count, first_row, group, h):
         def piece(b, hh):
@@ -239,7 +252,6 @@
         return v
 
     r32[0:3 * channels, :] = jnp.dot(wb[...], xg[...], preferred_element_type=F32)
-    spread(0)
     for h in range(height):
         part[pl.ds(h, channels, stride=height), :] = shifted(channels, 0, channels, h)
 
@@ -262,21 +274,18 @@
             rsend[k] = (block_of(flip(z, 2 * k)) + nrecv[k].astype(F32)).astype(BF)
             sums[k - 1].start()
 
-    for group in range(1, groups):
-        for k in range(group * per, (group + 1) * per):
+    for g in range(groups):
+        for k in range(max(begin[g], 1), begin[g + 1]):
             gathers[k].wait_recv()
             if k == chan - 1:
                 near[0].start()
             fill_source(k)
-        share(group)
-        if group == 1 and groups > 2:
-            spread(1)
-        elif group > 2:
-            spread(group - 1)
+        share(g)
+        if g < groups - 1:
+            spread(g)
 
     pass_on()
-    if groups > 1:
-        spread(groups - 1)
+    spread(groups - 1)
     r32[0:9 * pad, :] = jnp.dot(wf[...], x3[:, LANE:LANE + span], preferred_element_type=F32)
 
     def relay(a):
@@ -298,6 +307,11 @@
     for k in range(groups - 1):
         collect(k)
     gather_up(groups - 1)
+    pl.when(has_down)(pair[0].wait_recv)
+    pl.when(has_up)(pair[1].wait_recv)
+    out_ref[...] = (t32[1, 0:rows, :] + precv[0].astype(F32)
+                    + precv[1].astype(F32)).astype(BF)
+
     collect(groups - 1)
     for a in range(3):
         for b in range(3):
@@ -305,11 +319,6 @@
                 at = b * tall + a * some
                 wg_ref[(a * 3 + b) * 3 + c] = (
                     acc[at:at + blk, c * wide:c * wide + channels] * scale)
-
-    pl.when(has_down)(pair[0].wait_recv)
-    pl.when(has_up)(pair[1].wait_recv)
-    out_ref[...] = (t32[1, 0:rows, :] + precv[0].astype(F32)
-                    + precv[1].astype(F32)).astype(BF)
 
     for c in sums:
         c.wait_recv()
@@ -345,17 +354,17 @@
     assert planes == 1 and width == LANE
     pad = up_to(blk, 16)
     rows = blk * height
-    groups = min(chan, 4)
+    cuts = [chan // 2, chan // 4, chan // 4]
     scale = 1.0 / math.sqrt(planes * space * height * width)
     dma = pltpu.SemaphoreType.DMA
     vm = pltpu.VMEM
     some = up_to(blk, 8)
     ring = up_to(3 * some, 16)
     deep = ring * chan
-    per = chan // groups
     tall = ring
-    half = up_to(3 * (3 * some if per == 1 else per * ring), 2 * LANE) // 2
-    flat = up_to(per * ring, LANE)
+    flats = [up_to(n * ring, LANE) for n in cuts]
+    halves = [up_to(3 * n * ring, 2 * LANE) // 2 for n in cuts]
+    groups = len(cuts)
     wide = up_to(channels, LANE)
     shapes = (
         jax.ShapeDtypeStruct((rows, LANE), BF),
@@ -363,7 +372,7 @@
         jax.ShapeDtypeStruct((27, blk, channels), F32),
     )
     outs = pl.pallas_call(
-        functools.partial(kernel, space, chan, blk, pad, channels, height, groups, scale),
+        functools.partial(kernel, space, chan, blk, pad, channels, height, cuts, scale),
         out_shape=shapes,
         in_specs=[pl.BlockSpec(memory_space=pltpu.HBM)] * 3,
         out_specs=[pl.BlockSpec(memory_space=vm)] * 3,
@@ -383,14 +392,14 @@
             vm((2, rows, LANE), BF),
             vm((2, rows, LANE), BF),
             vm((2, rows, LANE), BF),
-            vm((groups, tall, 2 * half), F32),
-            vm((groups, tall, half), BF),
-            vm((groups, tall, half), BF),
-            vm((groups, space, tall, half), BF),
-            vm((groups, 2, tall, half), BF),
-            vm((3 * tall, flat), BF),
+            tuple(vm((tall, 2 * half), F32) for half in halves),
+            tuple(vm((tall, half), BF) for half in halves),
+            tuple(vm((tall, half), BF) for half in halves),
+            tuple(vm((space, tall, half), BF) for half in halves),
+            tuple(vm((2, tall, half), BF) for half in halves),
+            tuple(vm((3 * tall, flat), BF) for flat in flats),
             vm((3 * tall, 3 * wide), F32),
-            vm((groups, flat, 3 * wide), BF),
+            tuple(vm((flat, 3 * wide), BF) for flat in flats),
             vm((chan // 2, rows, LANE), BF),
             vm((chan // 2, rows, LANE), BF),
             vm((chan // 2, rows, LANE), BF),

time: 25 us -> 23.8 us (0.952)
  Pallas kernels: 24.2 us -> 23 us
    pallas_call x1, Pallas kernels: 23.4 us -> 22.2 us  [body(): pl.pallas_call(functools.partial(kernel, space, chan, blk, pad, channels,...]
where the time goes in v4:
time: 23.8 us; the launch traced here: 23.6 us
  Pallas kernels  23 us (97%)
  between operations  0.64 us (3%)
    pallas_call x1, Pallas kernels, body(): pl.pallas_call(functools.partial(kernel, space, chan, blk, pad, channels,...  22.2 us
    pallas_call x1, Pallas kernels, body(): pl.pallas_call(write, out_shape=shapes, in_specs=[pl.BlockSpec(memory_spa...  0.82 us

profile of v4, /device:TPU:0, one launch (start us, length us, event | category | flops | bytes accessed | tf_op | source)
XLA Modules:
  0.0 23.6 jit_solution(8187842595193535985)
XLA Ops:
  0.6 22.2 %shard_map.58 = (bf16[384,128]{1,0:T(8,128)(2,1)S(1)}, bf16[384,128]{1,0:T(8,128)(2,1)S(1)}, f32[27,24,96]{2,1,0:T(8,128)S(1)}) custom-call(bf16[384,128]{1,0:T(8,128)(2,1)} %bitcast.9, bf16[384,128]{1,0:T(8,128)(2,1)} %bitcast.10, bf16[27,96,96]{2,1,0:T(8,128)(2,1)} %bitcast.8), custom_call_target="tpu_custom_call" | custom-call | tf_op jit(solution)/shard_map/pallas_call | solution.py:374
  22.8 0.8 %shard_map.59 = (bf16[384,128]{1,0:T(8,128)(2,1)}, bf16[384,128]{1,0:T(8,128)(2,1)}, f32[27,24,96]{2,1,0:T(8,128)}) custom-call(bf16[384,128]{1,0:T(8,128)(2,1)S(1)} %get-tuple-element.9.refs_0_, bf16[384,128]{1,0:T(8,128)(2,1)S(1)} %get-tuple-element.10.refs_1_, f32[27,24,96]{2,1,0:T(8,128)S(1)} %get-tuple-element.11.refs_2_), custom_call_target="tpu_custom_call" | custom-call | tf_op jit(solution)/shard_map/pallas_call | solution.py:417

commit v5 on v4

--- a/solution.py
+++ b/solution.py
@@ -255,30 +255,55 @@
     for h in range(height):
         part[pl.ds(h, channels, stride=height), :] = shifted(channels, 0, channels, h)
 
-    near = [send(nsend.at[k], nrecv.at[k], n_s.at[k], n_r.at[k], {"chan": flip(z, 1)})
-            for k in range(chan // 2)]
-    sums = [send(rsend.at[k], rrecv.at[k], r_s.at[k], r_r.at[k], {"chan": flip(z, 2 * k)})
-            for k in range(1, chan // 2)]
-
     def block_of(t):
         return part[pl.ds(pl.multiple_of(t * rows, 16), rows), :]
 
-    for k in reversed(range(chan // 2)):
-        nsend[k] = block_of(flip(z, 2 * k + 1)).astype(BF)
-    for c in near[1:]:
-        c.start()
+    def on(where):
+        return lambda step: pl.when(where)(step)
+
+    always = lambda step: step()
+    if chan == 4:
+        inner = lax.rem(lax.div(z + 1, 2), 2) == 1
+        gives, takes = on(jnp.logical_not(inner)), on(inner)
+        given = [flip(z, 3), flip(z, 2)]
+        owners = [flip(z, 2), flip(z, 3)]
+        slots = [0, 0]
+    else:
+        gives = takes = always
+        given = [flip(z, 2 * k + 1) for k in range(1, chan // 2)]
+        owners = [flip(z, 2 * k) for k in range(1, chan // 2)]
+        slots = list(range(chan // 2 - 1))
+    next_z = {"chan": flip(z, 1)}
+    far = [send(nsend.at[k], nrecv.at[k], n_s.at[k], n_r.at[k], next_z)
+           for k in range(1, len(given) + 1)]
+    near = send(nsend.at[0], nrecv.at[0], n_s.at[0], n_r.at[0], next_z)
+    sums = [send(rsend.at[k], rrecv.at[slot], r_s.at[k], r_r.at[slot], {"chan": owner})
+            for k, (slot, owner) in enumerate(zip(slots, owners))]
+
+    def give():
+        for k, t in enumerate(given):
+            nsend[k + 1] = block_of(t).astype(BF)
+            far[k].start()
+
+    def take():
+        for k, owner in enumerate(owners):
+            far[k].wait_recv()
+            rsend[k] = (block_of(owner) + nrecv[k + 1].astype(F32)).astype(BF)
+            sums[k].start()
+
+    nsend[0] = block_of(flip(z, 1)).astype(BF)
+    gives(give)
 
     def pass_on():
-        for k in range(1, chan // 2):
-            near[k].wait_recv()
-            rsend[k] = (block_of(flip(z, 2 * k)) + nrecv[k].astype(F32)).astype(BF)
-            sums[k - 1].start()
+        takes(take)
 
     for g in range(groups):
         for k in range(max(begin[g], 1), begin[g + 1]):
             gathers[k].wait_recv()
-            if k == chan - 1:
-                near[0].start()
+            if k == chan - 2:
+                takes(near.start)
+            if k == chan - 1 and chan == 4:
+                gives(near.start)
             fill_source(k)
         share(g)
         if g < groups - 1:
@@ -320,16 +345,26 @@
                 wg_ref[(a * 3 + b) * 3 + c] = (
                     acc[at:at + blk, c * wide:c * wide + channels] * scale)
 
-    for c in sums:
-        c.wait_recv()
-    near[0].wait_recv()
+    near.wait_recv()
     total = block_of(z) + nrecv[0].astype(F32)
-    for k in range(1, chan // 2):
-        total = total + rrecv[k].astype(F32)
+    for slot in sorted(set(slots)):
+        sums[slot].wait_recv()
+        total = total + rrecv[slot].astype(F32)
     back_ref[...] = total.astype(BF)
 
-    for c in gathers[1:] + near + sums + pairs + passes:
+    for c in gathers[1:] + [near] + pairs + passes:
         c.wait_send()
+
+    def given_sent():
+        for c in far:
+            c.wait_send()
+
+    def sums_sent():
+        for c in sums:
+            c.wait_send()
+
+    gives(given_sent)
+    takes(sums_sent)
     for group in shares:
         for c in group:
             c.wait_send()
@@ -400,14 +435,14 @@
             tuple(vm((3 * tall, flat), BF) for flat in flats),
             vm((3 * tall, 3 * wide), F32),
             tuple(vm((flat, 3 * wide), BF) for flat in flats),
-            vm((chan // 2, rows, LANE), BF),
-            vm((chan // 2, rows, LANE), BF),
+            vm((chan // 2 + 1, rows, LANE), BF),
+            vm((chan // 2 + 1, rows, LANE), BF),
             vm((chan // 2, rows, LANE), BF),
             vm((chan // 2, rows, LANE), BF),
             dma((3,)), dma((chan,)), dma((chan,)), dma((2,)), dma((2,)), dma((2,)), dma((2,)),
             dma((groups,)), dma((groups,)), dma((groups, space)), dma((groups, space)),
             dma((groups,)), dma((groups,)),
-            dma((chan // 2,)), dma((chan // 2,)), dma((chan // 2,)), dma((chan // 2,)),
+            dma((chan // 2 + 1,)), dma((chan // 2 + 1,)), dma((chan // 2,)), dma((chan // 2,)),
         ],
         compiler_params=pltpu.CompilerParams(
             collective_id=0, has_side_effects=True, vmem_limit_bytes=40 * 2**20),

time: 23.8 us -> 23.7 us (level)
  no operation moved by 1% of the time
where the time goes in v5:
time: 23.7 us; the launch traced here: 23.6 us
  Pallas kernels  22.9 us (97%)
  between operations  0.64 us (3%)
    pallas_call x1, Pallas kernels, body(): pl.pallas_call(functools.partial(kernel, space, chan, blk, pad, channels,...  22.1 us
    pallas_call x1, Pallas kernels, body(): pl.pallas_call(write, out_shape=shapes, in_specs=[pl.BlockSpec(memory_spa...  0.82 us

profile of v5, /device:TPU:0, one launch (start us, length us, event | category | flops | bytes accessed | tf_op | source)
XLA Modules:
  0.0 23.6 jit_solution(208195998055182973)
XLA Ops:
  0.6 22.1 %shard_map.58 = (bf16[384,128]{1,0:T(8,128)(2,1)S(1)}, bf16[384,128]{1,0:T(8,128)(2,1)S(1)}, f32[27,24,96]{2,1,0:T(8,128)S(1)}) custom-call(bf16[384,128]{1,0:T(8,128)(2,1)} %bitcast.9, bf16[384,128]{1,0:T(8,128)(2,1)} %bitcast.10, bf16[27,96,96]{2,1,0:T(8,128)(2,1)} %bitcast.8), custom_call_target="tpu_custom_call" | custom-call | tf_op jit(solution)/shard_map/pallas_call | solution.py:409
  22.7 0.8 %shard_map.59 = (bf16[384,128]{1,0:T(8,128)(2,1)}, bf16[384,128]{1,0:T(8,128)(2,1)}, f32[27,24,96]{2,1,0:T(8,128)}) custom-call(bf16[384,128]{1,0:T(8,128)(2,1)S(1)} %get-tuple-element.9.refs_0_, bf16[384,128]{1,0:T(8,128)(2,1)S(1)} %get-tuple-element.10.refs_1_, f32[27,24,96]{2,1,0:T(8,128)S(1)} %get-tuple-element.11.refs_2_), custom_call_target="tpu_custom_call" | custom-call | tf_op jit(solution)/shard_map/pallas_call | solution.py:452

commit v6 on v5

--- a/solution.py
+++ b/solution.py
@@ -28,7 +28,7 @@
 
 def kernel(space, chan, blk, pad, channels, height, cuts, scale,
            a_hbm, g_hbm, w_hbm, out_ref, back_ref, wg_ref,
-           ga, gv, w_ref, x3, xg, wt, wf, wb, z32, t32, r32, part,
+           ga, gv, w_ref, x3, xs, xg, wt, wf, wb, z32, t32, r32, part,
            halo, psend, precv, wflat, csend, crecv, wall, full, stack, acc, place_q,
            nsend, nrecv, rsend, rrecv,
            l_s, g_s, g_r, h_s, h_r, p_s, p_r, c_s, c_r, w_s, w_r, f_s, f_r, n_s, n_r, r_s, r_r):
@@ -87,8 +87,9 @@
     pl.when(e == space - 1)(no_upper)
 
     z32[...] = jnp.zeros_like(z32)
-    x3[:, 0:LANE] = jnp.zeros((x3.shape[0], LANE), BF)
-    x3[:, span + LANE:span + 2 * LANE] = jnp.zeros((x3.shape[0], LANE), BF)
+    for g in range(groups):
+        xs[g][0:each[g], 0:LANE] = jnp.zeros((each[g], LANE), BF)
+        xs[g][2 * each[g]:3 * each[g], span - LANE:span] = jnp.zeros((each[g], LANE), BF)
     for ref in (*wflat, *stack, *place_q):
         ref[...] = jnp.zeros_like(ref)
     few = lax.broadcasted_iota(jnp.int32, (rows, LANE), 1)
@@ -109,11 +110,17 @@
 
     def fill_source(k):
         shift(ga[k])
+        g = max(g for g in range(groups) if begin[g] <= k)
         rest = [jnp.zeros((ring - 3 * some, LANE), F32)] if ring > 3 * some else []
         for h in range(height):
             taps = [z32[c, pl.ds(h, some, stride=height), :] for c in range(3)]
-            x3[k * ring:(k + 1) * ring, (h + 1) * LANE:(h + 2) * LANE] = (
-                jnp.concatenate(taps + rest, axis=0).astype(BF))
+            piece = jnp.concatenate(taps + rest, axis=0).astype(BF)
+            x3[k * ring:(k + 1) * ring, h * LANE:(h + 1) * LANE] = piece
+            for b in range(3):
+                to = h + 1 - b
+                if 0 <= to < height:
+                    at = b * each[g] + (k - begin[g]) * ring
+                    xs[g][at:at + ring, to * LANE:(to + 1) * LANE] = piece
 
     fill_signal(1, gv[...])
     fill_source(0)
@@ -189,14 +196,10 @@
         return wflat[g][:, pl.ds(pl.multiple_of(which * half, LANE), half)]
 
     def share(g):
-        for b in range(3):
-            one = lax.dot_general(
-                xg[3 * pad:6 * pad, :],
-                x3[begin[g] * ring:begin[g + 1] * ring, b * LANE:b * LANE + span],
-                ROWS_T, preferred_element_type=F32)
-            for a in range(3):
-                wflat[g][a * some:(a + 1) * some, b * each[g]:(b + 1) * each[g]] = (
-                    one[a * pad:a * pad + some, :])
+        one = lax.dot_general(
+            xg[3 * pad:6 * pad, :], xs[g][...], ROWS_T, preferred_element_type=F32)
+        for a in range(3):
+            wflat[g][a * some:(a + 1) * some, 0:3 * each[g]] = one[a * pad:a * pad + some, :]
         csend[g][...] = my_half(g, 1 - core).astype(BF)
         if g == last:
             wall[g][e] = my_half(g, core).astype(BF)
@@ -311,7 +314,7 @@
 
     pass_on()
     spread(groups - 1)
-    r32[0:9 * pad, :] = jnp.dot(wf[...], x3[:, LANE:LANE + span], preferred_element_type=F32)
+    r32[0:9 * pad, :] = jnp.dot(wf[...], x3[...], preferred_element_type=F32)
 
     def relay(a):
         for h in range(height):
@@ -377,7 +380,7 @@
 def write(*refs):
     n = len(refs) // 2
     copies = [pltpu.make_async_copy(refs[i], refs[n + i], refs[-1].at[i]) for i in range(n)]
-    for c in copies:
+    for c in reversed(copies):
         c.start()
     for c in copies:
         c.wait()
@@ -415,7 +418,8 @@
             vm((chan, rows, LANE), BF),
             vm((rows, LANE), BF),
             vm((27, channels, channels), BF),
-            vm((deep, (height + 2) * LANE), BF),
+            vm((deep, height * LANE), BF),
+            tuple(vm((3 * n * ring, height * LANE), BF) for n in cuts),
             vm((9 * pad, height * LANE), BF),
             vm((3, 9 * pad, channels), BF),
             vm((9 * pad, deep), BF),

time: 23.7 us -> 23.7 us (level)
  no operation moved by 1% of the time
where the time goes in v6:
time: 23.7 us; the launch traced here: 23.6 us
  Pallas kernels  22.9 us (97%)
  between operations  0.64 us (3%)
    pallas_call x1, Pallas kernels, body(): pl.pallas_call(functools.partial(kernel, space, chan, blk, pad, channels,...  22.1 us
    pallas_call x1, Pallas kernels, body(): pl.pallas_call(write, out_shape=shapes, in_specs=[pl.BlockSpec(memory_spa...  0.81 us

profile of v6, /device:TPU:0, one launch (start us, length us, event | category | flops | bytes accessed | tf_op | source)
XLA Modules:
  0.0 23.6 jit_solution(9112306144546422299)
XLA Ops:
  0.6 22.1 %shard_map.58 = (bf16[384,128]{1,0:T(8,128)(2,1)S(1)}, bf16[384,128]{1,0:T(8,128)(2,1)S(1)}, f32[27,24,96]{2,1,0:T(8,128)S(1)}) custom-call(bf16[384,128]{1,0:T(8,128)(2,1)} %bitcast.9, bf16[384,128]{1,0:T(8,128)(2,1)} %bitcast.10, bf16[27,96,96]{2,1,0:T(8,128)(2,1)} %bitcast.8), custom_call_target="tpu_custom_call" | custom-call | tf_op jit(solution)/shard_map/pallas_call | solution.py:412
  22.7 0.8 %shard_map.59 = (bf16[384,128]{1,0:T(8,128)(2,1)}, bf16[384,128]{1,0:T(8,128)(2,1)}, f32[27,24,96]{2,1,0:T(8,128)}) custom-call(bf16[384,128]{1,0:T(8,128)(2,1)S(1)} %get-tuple-element.9.refs_0_, bf16[384,128]{1,0:T(8,128)(2,1)S(1)} %get-tuple-element.10.refs_1_, f32[27,24,96]{2,1,0:T(8,128)S(1)} %get-tuple-element.11.refs_2_), custom_call_target="tpu_custom_call" | custom-call | tf_op jit(solution)/shard_map/pallas_call | solution.py:456

commit v7 on v5

--- a/solution.py
+++ b/solution.py
@@ -292,14 +292,14 @@
             sums[k].start()
 
     nsend[0] = block_of(flip(z, 1)).astype(BF)
-    gives(give)
-
     def pass_on():
         takes(take)
 
     for g in range(groups):
         for k in range(max(begin[g], 1), begin[g + 1]):
             gathers[k].wait_recv()
+            if k == 1:
+                gives(give)
             if k == chan - 2:
                 takes(near.start)
             if k == chan - 1 and chan == 4:

time: 23.7 us -> 23.7 us (level)
  no operation moved by 1% of the time
where the time goes in v7:
time: 23.7 us; the launch traced here: 23.5 us
  Pallas kernels  22.8 us (96%)
  between operations  0.64 us (3%)
    pallas_call x1, Pallas kernels, body(): pl.pallas_call(functools.partial(kernel, space, chan, blk, pad, channels,...  22 us
    pallas_call x1, Pallas kernels, body(): pl.pallas_call(write, out_shape=shapes, in_specs=[pl.BlockSpec(memory_spa...  0.82 us

profile of v7, /device:TPU:0, one launch (start us, length us, event | category | flops | bytes accessed | tf_op | source)
XLA Modules:
  0.0 23.5 jit_solution(18397402536436798436)
XLA Ops:
  0.6 22.0 %shard_map.58 = (bf16[384,128]{1,0:T(8,128)(2,1)S(1)}, bf16[384,128]{1,0:T(8,128)(2,1)S(1)}, f32[27,24,96]{2,1,0:T(8,128)S(1)}) custom-call(bf16[384,128]{1,0:T(8,128)(2,1)} %bitcast.9, bf16[384,128]{1,0:T(8,128)(2,1)} %bitcast.10, bf16[27,96,96]{2,1,0:T(8,128)(2,1)} %bitcast.8), custom_call_target="tpu_custom_call" | custom-call | tf_op jit(solution)/shard_map/pallas_call | solution.py:409
  22.6 0.8 %shard_map.59 = (bf16[384,128]{1,0:T(8,128)(2,1)}, bf16[384,128]{1,0:T(8,128)(2,1)}, f32[27,24,96]{2,1,0:T(8,128)}) custom-call(bf16[384,128]{1,0:T(8,128)(2,1)S(1)} %get-tuple-element.9.refs_0_, bf16[384,128]{1,0:T(8,128)(2,1)S(1)} %get-tuple-element.10.refs_1_, f32[27,24,96]{2,1,0:T(8,128)S(1)} %get-tuple-element.11.refs_2_), custom_call_target="tpu_custom_call" | custom-call | tf_op jit(solution)/shard_map/pallas_call | solution.py:452
